TPU v7x, 256 devices: a whole 4x4x8 slice. The times are simulated.
256 devices in a mesh: ex: 32 (over x_lo, z, core), layer: 8 (over x_hi, y).
Axes of the slice: x: 4 (x_hi: 2, x_lo: 2; x = x_hi * 2 + x_lo), y: 4, z: 8, core: 2. Of those that a mesh axis runs over, the one named last changes fastest.
Arguments:
- activations: bfloat16 [8, 64, 256, 11008], P('layer', 'ex'), may hold values from -6 to 6
- grad_proj: float32 [8, 64, 64, 256], P('layer', 'ex'), may hold values from -6 to 6
- proj_in: bfloat16 [8, 64, 11008], P('layer'), may hold values from -0.0546875 to 0.0546875
Outputs:
- gram: float32 [64, 64], P('ex', 'layer')
All inputs are finite; a program needn't handle non-finite values.
Results may differ from a plain program's by a relative error of at most 0.0003.
Values sent between devices are 32-bit elements; how exact they have to be, the bound alone decides.
No kernel may reach another device: no remote copies, remote signals or barrier semaphores. Data moves between devices by JAX's collectives and lax.ppermute only.
A program may use at most 64 MiB of HBM per device.

v0:
```python
import math

import jax
import jax.numpy as jnp
from jax import lax
from jax.sharding import PartitionSpec as P


def inner_rows(left, right):
    return lax.dot_general(
        left,
        right,
        (((1,), (1,)), ((), ())),
        precision=lax.Precision.HIGHEST,
        preferred_element_type=jnp.float32,
    )


def shards(activations, grad_proj, proj_in):
    count = activations.shape[1]
    seq_len = activations.shape[2]
    rank = proj_in.shape[1]
    flat = activations[0].reshape(count * seq_len, activations.shape[3])
    px = lax.dot_general(
        flat, proj_in[0], (((1,), (1,)), ((), ())), preferred_element_type=jnp.float32
    )
    px = px.reshape(count, seq_len, rank)
    feats = jnp.einsum("eas,esb->eab", grad_proj[0], px, precision=lax.Precision.HIGHEST)
    feats = feats.reshape(count, rank * rank) * (1.0 / math.sqrt(seq_len))
    partial_value = inner_rows(feats, lax.all_gather(feats, "ex", axis=0, tiled=True))
    depth = lax.axis_size("layer")
    summed = lax.psum_scatter(partial_value, "layer", scatter_dimension=1, tiled=True)
    return summed * (1.0 / math.sqrt(depth * rank * rank))


def solution(mesh):
    return jax.shard_map(
        shards,
        mesh=mesh,
        in_specs=(
            P("layer", "ex", None, None),
            P("layer", "ex", None, None),
            P("layer", None, None),
        ),
        out_specs=P("ex", "layer"),
        check_vma=False,
    )
```

profile of v0, /device:TPU:1, one launch (start us, length us, event | category | flops | bytes accessed | tf_op | source)
XLA Modules:
  0.0 115.1 jit_solution(9343784479165158869)
XLA Ops:
  6.5 0.0 copy-start
  6.5 0.0 copy-start.2
  6.5 0.0 copy-start.1
  6.5 0.0 all-gather.3.cloned.1.call-start
  6.5 1.4 %copy-done = bf16[1,64,11008]{2,1,0:T(8,128)(2,1)S(1)} copy-done((bf16[1,64,11008]{2,1,0:T(8,128)(2,1)S(1)}, bf16[1,64,11008]{2,1,0:T(8,128)(2,1)}, u32[]{:S(2)}) %copy-start) | copy-done | bytes 1409048
  7.9 7.7 %fusion = f32[2,256,64]{1,2,0:T(8,128)S(1)} fusion(bf16[1,2,256,11008]{3,2,1,0:T(8,128)(2,1)} %param.3, bf16[1,64,11008]{2,1,0:T(8,128)(2,1)S(1)} %copy-done), kind=kOutput, calls=%fused_computation | convolution fusion | flops 721420288 | bytes 12812288 | tf_op jit(solution)/shard_map/dot_general | solution.py:24
  15.6 0.0 copy-done.1
  15.6 0.3 fusion.3
  15.9 0.1 copy.6
  16.0 0.7 reshape.6
  16.7 0.0 all-gather.3.cloned.1.call-update
  16.7 0.1 mul.18
  16.8 0.0 copy-done.2
  16.8 0.6 dynamic-slice
  18.1 66.6 %all-gather.3.cloned.1.call-done = f32[32,2,4096]{2,1,0:T(2,128)} async-done(((f32[1,2,4096]{2,1,0:T(2,128)}), f32[32,2,4096]{2,1,0:T(2,128)}) %all-gather.3.cloned.1.call-update) | async-done | bytes 1048592 | tf_op jit(solution)/shard_map/all_gather | solution.py:30
  84.7 1.9 %reshape.7 = f32[64,4096]{1,0:T(8,128)S(1)} reshape(f32[32,2,4096]{2,1,0:T(2,128)} %all-gather.3.cloned.1.call-done) | data formatting | bytes 2097152
  86.6 0.9 fusion.5
  87.5 20.1 %all-reduce = f32[2,64]{1,0:T(2,128)S(1)} all-reduce(f32[2,64]{1,0:T(2,128)S(1)} %fusion.5), channel_id=2, replica_groups=mesh['ex'=32,'layer'=8] {'layer'}, use_global_device_ids=true, to_apply=%region_0.0.clone | all-reduce | flops 128 | bytes 1024
  107.6 0.6 dynamic-slice_multiply_fusion
Async XLA Ops:
  6.5 1.4 %copy-start = (bf16[1,64,11008]{2,1,0:T(8,128)(2,1)S(1)}, bf16[1,64,11008]{2,1,0:T(8,128)(2,1)}, u32[]{:S(2)}) copy-start(bf16[1,64,11008]{2,1,0:T(8,128)(2,1)} %param.5) | copy-start | bytes 4227076
  6.5 10.3 %copy-start.2 = (u32[256]{0:T(256)S(1)}, u32[256]{0:T(256)}, u32[]{:S(2)}) copy-start(u32[256]{0:T(256)} %constant.9) | copy-start | bytes 3076
  6.5 9.1 %copy-start.1 = (f32[1,2,64,256]{3,2,1,0:T(8,128)S(1)}, f32[1,2,64,256]{3,2,1,0:T(8,128)}, u32[]{:S(2)}) copy-start(f32[1,2,64,256]{3,2,1,0:T(8,128)} %param.4) | copy-start | bytes 393220
  6.5 78.1 %all-gather.3.cloned.1.call-start = ((), (), s32[]{:S(2)}) async-start(), calls=%async_computation | async-start | bytes 1081344 | tf_op jit(solution)/shard_map/all_gather | solution.py:30
Sparse Core Ops, SparseCore 0:
  16.8 67.7 all-gather.2
where the time goes:
time: 117 us; the launch traced here: 115 us
  waiting for transfers between devices  66.6 us (57%)
  blocking collectives  20.1 us (17%)
  between operations  14.1 us (12%)
  matrix products  8.85 us (8%)
  local copies, waits for them, and re-layouts  4.81 us (4%)
    all_gather x1, waiting for transfers between devices, shards(): lax.all_gather(feats, 'ex', axis=0, tiled=True)  66.6 us
    unnamed x1, blocking collectives  20.1 us
    dot_general x1, matrix products, shards(): lax.dot_general(flat, proj_in[0], (((1,), (1,)), ((), ())), preferred_ele...  7.68 us
    unnamed x9, local copies, waits for them, and re-layouts  4.64 us
  transfers between devices with their start and end apart: 1, of which 1 were waited for; matrix products, arithmetic and copies ran while one was open for 1% of the time, Pallas kernels for 0%

commit v1 on v0

v1 whole, which is shorter than its diff:
```python
import math

import jax
import jax.numpy as jnp
from jax import lax
from jax.experimental import pallas as pl
from jax.experimental.pallas import tpu as pltpu
from jax.sharding import PartitionSpec as P

F32, BF16 = jnp.float32, jnp.bfloat16
LANES = 128
BLOCK = 1024
WINDOW = 3
Z_BITS = 1
VMEM_BYTES = 60 * 2**20
GRAM_VMEM = 8 * 2**20


def split3(x):
    high = x.astype(BF16)
    rest = x - high.astype(F32)
    mid = rest.astype(BF16)
    low = (rest - mid.astype(F32)).astype(BF16)
    return high, mid, low


def sum_blocks(product, rows, columns):
    total = None
    for order in (4, 3, 2, 1, 0):
        for i in range(3):
            j = order - i
            if 0 <= j < 3:
                block = product[i * rows : (i + 1) * rows, j * columns : (j + 1) * columns]
                total = block if total is None else total + block
    return total


def blocks_of(width):
    return [(at, min(BLOCK, width - at)) for at in range(0, width, BLOCK)]


def features_kernel(parts, acts, proj, grads, out, acts_buf, proj_buf, grads_buf, px, packed, acts_sem, proj_sem, grads_sem):
    count, rank, seq = grads.shape
    blocks = blocks_of(acts.shape[1])
    copies = []
    for n, (at, width) in enumerate(blocks):
        cut = pl.ds(at, width)
        copies.append((
            pltpu.make_async_copy(proj.at[:, cut], proj_buf.at[:, cut], proj_sem.at[n]),
            pltpu.make_async_copy(acts.at[:, cut], acts_buf.at[:, cut], acts_sem.at[n]),
        ))
    grads_copy = pltpu.make_async_copy(grads, grads_buf, grads_sem)
    for pair in copies[:WINDOW]:
        for copy in pair:
            copy.start()
    grads_copy.start()
    for n, (at, width) in enumerate(blocks):
        for copy in copies[n]:
            copy.wait()
        if n + WINDOW < len(blocks):
            for copy in copies[n + WINDOW]:
                copy.start()
        cut = pl.ds(at, width)
        term = lax.dot_general(
            acts_buf[:, cut], proj_buf[:, cut], (((1,), (1,)), ((), ())), preferred_element_type=F32
        )
        if n == 0:
            px[...] = term
        else:
            px[...] += term
    grads_copy.wait()
    half = rank // 2
    deep = half // parts
    for e in range(count):
        left = jnp.concatenate(split3(grads_buf[e]), axis=0)
        right = jnp.concatenate(split3(px[e * seq : (e + 1) * seq]), axis=1)
        feats = sum_blocks(jnp.dot(left, right, preferred_element_type=F32), rank, rank)
        feats = jnp.concatenate([feats[:half], feats[half:]], axis=1)
        for part in range(parts):
            packed[part, e * deep : (e + 1) * deep] = feats[part * deep : (part + 1) * deep]
    side = parts // 2
    for dest in range(out.shape[0]):
        part = dest // 16 * side + dest % side
        out[dest] = packed[part]


def features(parts, acts, proj, grads):
    count, rank, seq = grads.shape
    rows, width = acts.shape
    steps = len(blocks_of(width))
    deep = count * rank // 2 // parts
    anywhere = pl.BlockSpec(memory_space=pl.ANY)
    return pl.pallas_call(
        lambda *refs: features_kernel(parts, *refs),
        out_shape=jax.ShapeDtypeStruct((32, deep, 2 * rank), F32),
        in_specs=[anywhere] * 3,
        out_specs=pl.BlockSpec(memory_space=pltpu.VMEM),
        scratch_shapes=[
            pltpu.VMEM((rows, width), BF16),
            pltpu.VMEM((rank, width), BF16),
            pltpu.VMEM((count, rank, seq), F32),
            pltpu.VMEM((rows, rank), F32),
            pltpu.VMEM((parts, deep, 2 * rank), F32),
            pltpu.SemaphoreType.DMA((steps,)),
            pltpu.SemaphoreType.DMA((steps,)),
            pltpu.SemaphoreType.DMA,
        ],
        compiler_params=pltpu.CompilerParams(vmem_limit_bytes=VMEM_BYTES),
        name="features",
    )(acts, proj, grads)


def gram_kernel(parts, deep, feats, out, gram):
    examples = gram.shape[0]
    rows = jnp.concatenate(
        [feats[pl.ds(r, examples, stride=deep), :] for r in range(deep)], axis=1
    )
    terms = jnp.concatenate(split3(rows), axis=0)
    product = lax.dot_general(terms, terms, (((1,), (1,)), ((), ())), preferred_element_type=F32)
    gram[...] = sum_blocks(product, examples, examples)
    side = parts // 2
    group = lax.rem(lax.axis_index("ex"), 16) // side
    tall = 2 * side
    for x in range(2):
        mine = gram[pl.ds(x * 32 + group * tall, tall), :]
        for column in range(out.shape[0]):
            out[column, x * tall : (x + 1) * tall] = mine[:, column * 8 : (column + 1) * 8]


def gram_terms(parts, feats):
    sources, deep, lanes = feats.shape
    examples = 2 * sources
    return pl.pallas_call(
        lambda *refs: gram_kernel(parts, deep // 2, *refs),
        out_shape=jax.ShapeDtypeStruct((8, 2 * parts, 8), F32),
        in_specs=[pl.BlockSpec(memory_space=pltpu.VMEM)],
        out_specs=pl.BlockSpec(memory_space=pltpu.VMEM),
        scratch_shapes=[pltpu.VMEM((examples, examples), F32)],
        compiler_params=pltpu.CompilerParams(vmem_limit_bytes=GRAM_VMEM),
        name="gram_terms",
    )(feats.reshape(sources * deep, lanes))


def shards(activations, grad_proj, proj_in):
    _, count, seq, width = activations.shape
    rank = proj_in.shape[1]
    depth = lax.axis_size("layer")
    side = 2 << Z_BITS
    parts = 2 * side
    feats = features(parts, activations.reshape(count * seq, width), proj_in[0], grad_proj[0])
    feats = lax.all_to_all(feats, "ex", 0, 0, tiled=True)
    terms = gram_terms(parts, feats).reshape(8 * parts, 2, 8)
    groups = [
        [(x * 16 + z * side + w) * depth + layer for layer in range(depth) for x in range(2) for w in range(side)]
        for z in range(16 // side)
    ]
    terms = lax.all_to_all(terms, ("ex", "layer"), 0, 0, axis_index_groups=groups, tiled=True)
    return jnp.sum(terms, axis=0) * (1.0 / (seq * math.sqrt(depth * rank * rank)))


def solution(mesh):
    return jax.shard_map(
        shards,
        mesh=mesh,
        in_specs=(
            P("layer", "ex", None, None),
            P("layer", "ex", None, None),
            P("layer", None, None),
        ),
        out_specs=P("ex", "layer"),
        check_vma=False,
    )
```

time: 117 us -> 46.4 us (0.40); the launches traced: 115 us -> 46.2 us
  waiting for transfers between devices: 66.6 us -> 0 us
  blocking collectives: 20.1 us -> 37.1 us
  between operations: 14.1 us -> 0.01 us
  matrix products: 8.85 us -> 0 us
  Pallas kernels: 0 us -> 8.42 us
  local copies, waits for them, and re-layouts: 4.81 us -> 0 us
    all_gather x1 -> x0, waiting for transfers between devices: 66.6 us -> none  [shards(): lax.all_gather(feats, 'ex', axis=0, tiled=True)]
    all_to_all x0 -> x2, blocking collectives: none -> 37.1 us  [the longest x1 20.1 us: shards(): feats = lax.all_to_all(feats, 'ex', 0, 0, tiled=True)]
    unnamed x1 -> x0, blocking collectives: 20.1 us -> none
    dot_general x3 -> x0, matrix products: 8.85 us -> none  [the longest x1 7.68 us: shards(): lax.dot_general(flat, proj_in[0], (((1,), (1,)), ((), ())), preferred_ele...]
    pallas_call x0 -> x2, Pallas kernels: none -> 8.42 us  [the longest x1 8.05 us: features(): pl.pallas_call(lambda *refs: features_kernel(parts, *refs), out_shape=jax...]
    unnamed x9 -> x0, local copies, waits for them, and re-layouts: 4.64 us -> none
  transfers between devices with their start and end apart: 1 -> 0, of which waited for: 1 -> 0; matrix products, arithmetic and copies ran while one was open for 1% -> 0% of each run, Pallas kernels for 0% -> 0%
where the time goes in v1:
time: 46.4 us; the launch traced here: 46.2 us
  blocking collectives  37.1 us (80%)
  Pallas kernels  8.42 us (18%)
  other arithmetic  0.65 us (1%)
    all_to_all x1, blocking collectives, shards(): feats = lax.all_to_all(feats, 'ex', 0, 0, tiled=True)  20.1 us
    all_to_all x1, blocking collectives, shards(): lax.all_to_all(terms, ('ex', 'layer'), 0, 0, axis_index_groups=groups, ti...  17 us
    pallas_call x1, Pallas kernels, features(): pl.pallas_call(lambda *refs: features_kernel(parts, *refs), out_shape=jax...  8.05 us

profile of v1, /device:TPU:1, one launch (start us, length us, event | category | flops | bytes accessed | tf_op | source)
XLA Modules:
  0.0 46.2 jit_solution(14125448840463522392)
XLA Ops:
  0.0 8.0 %features.1 = f32[32,8,128]{2,1,0:T(8,128)} custom-call(bf16[512,11008]{1,0:T(8,128)(2,1)} %bitcast.7, bf16[64,11008]{1,0:T(8,128)(2,1)} %bitcast.8, f32[2,64,256]{2,1,0:T(8,128)} %bitcast.9), custom_call_target="tpu_custom_call" | custom-call | tf_op jit(solution)/shard_map/features/pallas_call | solution.py:93
  8.1 20.1 %all_to_all.10 = f32[32,8,128]{2,1,0:T(8,128)S(1)} all-to-all(f32[32,8,128]{2,1,0:T(8,128)} %features.1), channel_id=1, replica_groups=mesh['ex'=32,'layer'=8] {'ex'}, dimensions={0} | all-to-all | bytes 262144 | tf_op jit(solution)/shard_map/all_to_all | solution.py:151
  28.2 0.4 gram_terms.1
  28.6 17.0 %all_to_all.11 = f32[64,2,8]{2,1,0:T(2,128)S(1)} all-to-all(f32[64,2,8]{2,1,0:T(2,128)S(1)} %bitcast.6), channel_id=1, replica_groups={{0,8,16,24,128,136,144,152,1,9,17,25,129,137,145,153,2,10,18,26,130,138..., dimensions={0} | all-to-all | bytes 8192 | tf_op jit(solution)/shard_map/all_to_all | solution.py:157
  45.5 0.1 reduce_sum.9
  45.6 0.6 %broadcast_multiply_fusion = f32[2,8]{1,0:T(2,128)} fusion(f32[2,8]{1,0:T(2,128)S(1)} %reduce_sum.9), kind=kLoop, calls=%fused_computation | loop fusion | flops 16 | bytes 128 | tf_op jit(solution)/shard_map/mul | solution.py:158

commit v2 on v1

--- a/solution.py
+++ b/solution.py
@@ -2,6 +2,7 @@
 
 import jax
 import jax.numpy as jnp
+import numpy as np
 from jax import lax
 from jax.experimental import pallas as pl
 from jax.experimental.pallas import tpu as pltpu
@@ -9,10 +10,10 @@
 
 F32, BF16 = jnp.float32, jnp.bfloat16
 LANES = 128
-BLOCK = 1024
-WINDOW = 3
+FIRST, LARGE, LAST = 4, 16, (12, 6)
+WINDOW = 7
 Z_BITS = 1
-VMEM_BYTES = 60 * 2**20
+VMEM_BYTES = 16 * 2**20
 GRAM_VMEM = 8 * 2**20
 
 
@@ -36,7 +37,10 @@
 
 
 def blocks_of(width):
-    return [(at, min(BLOCK, width - at)) for at in range(0, width, BLOCK)]
+    left = width // LANES - FIRST - sum(LAST)
+    tiles = [FIRST] + [LARGE] * (left // LARGE) + [left % LARGE] * (left % LARGE > 0) + list(LAST)
+    ends = np.cumsum(tiles) * LANES
+    return [(int(end) - tile * LANES, tile * LANES) for end, tile in zip(ends, tiles)]
 
 
 def features_kernel(parts, acts, proj, grads, out, acts_buf, proj_buf, grads_buf, px, packed, acts_sem, proj_sem, grads_sem):
@@ -92,7 +96,7 @@
     anywhere = pl.BlockSpec(memory_space=pl.ANY)
     return pl.pallas_call(
         lambda *refs: features_kernel(parts, *refs),
-        out_shape=jax.ShapeDtypeStruct((32, deep, 2 * rank), F32),
+        out_shape=pltpu.VMEM((32, deep, 2 * rank), F32),
         in_specs=[anywhere] * 3,
         out_specs=pl.BlockSpec(memory_space=pltpu.VMEM),
         scratch_shapes=[
@@ -107,17 +111,17 @@
         ],
         compiler_params=pltpu.CompilerParams(vmem_limit_bytes=VMEM_BYTES),
         name="features",
-    )(acts, proj, grads)
+    )(*(pltpu.with_memory_space_constraint(x, pltpu.HBM) for x in (acts, proj, grads)))
 
 
-def gram_kernel(parts, deep, feats, out, gram):
+def gram_kernel(parts, deep, scale, feats, out, gram):
     examples = gram.shape[0]
     rows = jnp.concatenate(
         [feats[pl.ds(r, examples, stride=deep), :] for r in range(deep)], axis=1
     )
     terms = jnp.concatenate(split3(rows), axis=0)
     product = lax.dot_general(terms, terms, (((1,), (1,)), ((), ())), preferred_element_type=F32)
-    gram[...] = sum_blocks(product, examples, examples)
+    gram[...] = sum_blocks(product, examples, examples) * scale
     side = parts // 2
     group = lax.rem(lax.axis_index("ex"), 16) // side
     tall = 2 * side
@@ -127,11 +131,11 @@
             out[column, x * tall : (x + 1) * tall] = mine[:, column * 8 : (column + 1) * 8]
 
 
-def gram_terms(parts, feats):
+def gram_terms(parts, scale, feats):
     sources, deep, lanes = feats.shape
     examples = 2 * sources
     return pl.pallas_call(
-        lambda *refs: gram_kernel(parts, deep // 2, *refs),
+        lambda *refs: gram_kernel(parts, deep // 2, scale, *refs),
         out_shape=jax.ShapeDtypeStruct((8, 2 * parts, 8), F32),
         in_specs=[pl.BlockSpec(memory_space=pltpu.VMEM)],
         out_specs=pl.BlockSpec(memory_space=pltpu.VMEM),
@@ -149,13 +153,14 @@
     parts = 2 * side
     feats = features(parts, activations.reshape(count * seq, width), proj_in[0], grad_proj[0])
     feats = lax.all_to_all(feats, "ex", 0, 0, tiled=True)
-    terms = gram_terms(parts, feats).reshape(8 * parts, 2, 8)
+    scale = 1.0 / (seq * math.sqrt(depth * rank * rank))
+    terms = gram_terms(parts, scale, feats).reshape(8 * parts, 2, 8)
     groups = [
         [(x * 16 + z * side + w) * depth + layer for layer in range(depth) for x in range(2) for w in range(side)]
         for z in range(16 // side)
     ]
     terms = lax.all_to_all(terms, ("ex", "layer"), 0, 0, axis_index_groups=groups, tiled=True)
-    return jnp.sum(terms, axis=0) * (1.0 / (seq * math.sqrt(depth * rank * rank)))
+    return jnp.sum(terms, axis=0)
 
 
 def solution(mesh):

time: 46.4 us -> 44.4 us (0.957)
  Pallas kernels: 8.42 us -> 6.76 us
    pallas_call x2, Pallas kernels: 8.42 us -> 6.76 us  [the longest x1 6.38 us: features(): pl.pallas_call(lambda *refs: features_kernel(parts, *refs), out_shape=plt...]
    mul x1 -> x0, other arithmetic: 0.57 us -> none  [shards(): jnp.sum(terms, axis=0) * (1.0 / (seq * math.sqrt(depth * rank * rank)))]
    reduce_sum x1, other arithmetic: 0.08 us -> 0.64 us  [shards(): return jnp.sum(terms, axis=0)]
where the time goes in v2:
time: 44.4 us; the launch traced here: 44.3 us
  blocking collectives  36.9 us (83%)
  Pallas kernels  6.76 us (15%)
  other arithmetic  0.64 us (1%)
    all_to_all x1, blocking collectives, shards(): feats = lax.all_to_all(feats, 'ex', 0, 0, tiled=True)  19.9 us
    all_to_all x1, blocking collectives, shards(): lax.all_to_all(terms, ('ex', 'layer'), 0, 0, axis_index_groups=groups, ti...  17 us
    pallas_call x1, Pallas kernels, features(): pl.pallas_call(lambda *refs: features_kernel(parts, *refs), out_shape=plt...  6.38 us

profile of v2, /device:TPU:1, one launch (start us, length us, event | category | flops | bytes accessed | tf_op | source)
XLA Modules:
  0.0 44.3 jit_solution(16279247178327029793)
XLA Ops:
  0.0 6.4 %features.1 = f32[32,8,128]{2,1,0:T(8,128)S(1)} custom-call(bf16[512,11008]{1,0:T(8,128)(2,1)} %bitcast.7, bf16[64,11008]{1,0:T(8,128)(2,1)} %bitcast.8, f32[2,64,256]{2,1,0:T(8,128)} %bitcast.9), custom_call_target="tpu_custom_call" | custom-call | tf_op jit(solution)/shard_map/features/pallas_call | solution.py:97
  6.4 19.9 %all_to_all.10 = f32[32,8,128]{2,1,0:T(8,128)S(1)} all-to-all(f32[32,8,128]{2,1,0:T(8,128)S(1)} %features.1), channel_id=1, replica_groups=mesh['ex'=32,'layer'=8] {'ex'}, dimensions={0} | all-to-all | bytes 262144 | tf_op jit(solution)/shard_map/all_to_all | solution.py:155
  26.3 0.4 gram_terms.1
  26.7 17.0 %all_to_all.11 = f32[64,2,8]{2,1,0:T(2,128)S(1)} all-to-all(f32[64,2,8]{2,1,0:T(2,128)S(1)} %bitcast.6), channel_id=1, replica_groups={{0,8,16,24,128,136,144,152,1,9,17,25,129,137,145,153,2,10,18,26,130,138..., dimensions={0} | all-to-all | bytes 8192 | tf_op jit(solution)/shard_map/all_to_all | solution.py:162
  43.7 0.6 %reduce_sum.9 = f32[2,8]{1,0:T(2,128)} reduce(f32[64,2,8]{2,1,0:T(2,128)S(1)} %all_to_all.11, f32[]{:T(128)} %constant.0.clone.1), dimensions={0}, to_apply=%region_0.0 | reduce | flops 1008 | bytes 4164 | tf_op jit(solution)/shard_map/reduce_sum | solution.py:163

commit v3 on v2

--- a/solution.py
+++ b/solution.py
@@ -15,6 +15,14 @@
 Z_BITS = 1
 VMEM_BYTES = 16 * 2**20
 GRAM_VMEM = 8 * 2**20
+
+
+def first_order():
+    return list(reversed(range(32)))
+
+
+def second_order(parts):
+    return [(layer, part) for layer in reversed(range(8)) for part in reversed(range(parts))]
 
 
 def split3(x):
@@ -43,7 +51,11 @@
     return [(int(end) - tile * LANES, tile * LANES) for end, tile in zip(ends, tiles)]
 
 
-def features_kernel(parts, acts, proj, grads, out, acts_buf, proj_buf, grads_buf, px, packed, acts_sem, proj_sem, grads_sem):
+def product_of(left, right):
+    return lax.dot_general(left, right, (((1,), (1,)), ((), ())), preferred_element_type=F32)
+
+
+def features_kernel(parts, acts, proj, grads, out, acts_buf, proj_buf, grads_buf, px, px_t, packed, acts_sem, proj_sem, grads_sem):
     count, rank, seq = grads.shape
     blocks = blocks_of(acts.shape[1])
     copies = []
@@ -54,10 +66,11 @@
             pltpu.make_async_copy(acts.at[:, cut], acts_buf.at[:, cut], acts_sem.at[n]),
         ))
     grads_copy = pltpu.make_async_copy(grads, grads_buf, grads_sem)
-    for pair in copies[:WINDOW]:
+    for n, pair in enumerate(copies[:WINDOW]):
         for copy in pair:
             copy.start()
-    grads_copy.start()
+        if n == 1:
+            grads_copy.start()
     for n, (at, width) in enumerate(blocks):
         for copy in copies[n]:
             copy.wait()
@@ -65,27 +78,31 @@
             for copy in copies[n + WINDOW]:
                 copy.start()
         cut = pl.ds(at, width)
-        term = lax.dot_general(
-            acts_buf[:, cut], proj_buf[:, cut], (((1,), (1,)), ((), ())), preferred_element_type=F32
-        )
-        if n == 0:
-            px[...] = term
-        else:
-            px[...] += term
+        first, second = acts_buf[:seq, cut], acts_buf[seq:, cut]
+        weights = proj_buf[:, cut]
+        terms = product_of(first, weights), product_of(weights, second)
+        for total, term in zip((px, px_t), terms):
+            if n == 0:
+                total[...] = term
+            else:
+                total[...] += term
     grads_copy.wait()
     half = rank // 2
     deep = half // parts
     for e in range(count):
         left = jnp.concatenate(split3(grads_buf[e]), axis=0)
-        right = jnp.concatenate(split3(px[e * seq : (e + 1) * seq]), axis=1)
-        feats = sum_blocks(jnp.dot(left, right, preferred_element_type=F32), rank, rank)
+        if e == 0:
+            product = jnp.dot(left, jnp.concatenate(split3(px[...]), axis=1), preferred_element_type=F32)
+        else:
+            product = product_of(left, jnp.concatenate(split3(px_t[...]), axis=0))
+        feats = sum_blocks(product, rank, rank)
         feats = jnp.concatenate([feats[:half], feats[half:]], axis=1)
         for part in range(parts):
             packed[part, e * deep : (e + 1) * deep] = feats[part * deep : (part + 1) * deep]
     side = parts // 2
-    for dest in range(out.shape[0]):
+    for rank_in_group, dest in enumerate(first_order()):
         part = dest // 16 * side + dest % side
-        out[dest] = packed[part]
+        out[rank_in_group] = packed[part]
 
 
 def features(parts, acts, proj, grads):
@@ -103,7 +120,8 @@
             pltpu.VMEM((rows, width), BF16),
             pltpu.VMEM((rank, width), BF16),
             pltpu.VMEM((count, rank, seq), F32),
-            pltpu.VMEM((rows, rank), F32),
+            pltpu.VMEM((seq, rank), F32),
+            pltpu.VMEM((rank, seq), F32),
             pltpu.VMEM((parts, deep, 2 * rank), F32),
             pltpu.SemaphoreType.DMA((steps,)),
             pltpu.SemaphoreType.DMA((steps,)),
@@ -114,8 +132,11 @@
     )(*(pltpu.with_memory_space_constraint(x, pltpu.HBM) for x in (acts, proj, grads)))
 
 
-def gram_kernel(parts, deep, scale, feats, out, gram):
+def gram_kernel(parts, deep, scale, received, out, feats, gram):
     examples = gram.shape[0]
+    tile = 2 * deep
+    for rank_in_group, source in enumerate(first_order()):
+        feats[source * tile : (source + 1) * tile] = received[rank_in_group * tile : (rank_in_group + 1) * tile]
     rows = jnp.concatenate(
         [feats[pl.ds(r, examples, stride=deep), :] for r in range(deep)], axis=1
     )
@@ -125,10 +146,12 @@
     side = parts // 2
     group = lax.rem(lax.axis_index("ex"), 16) // side
     tall = 2 * side
-    for x in range(2):
-        mine = gram[pl.ds(x * 32 + group * tall, tall), :]
-        for column in range(out.shape[0]):
-            out[column, x * tall : (x + 1) * tall] = mine[:, column * 8 : (column + 1) * 8]
+    mine = jnp.concatenate(
+        [gram[pl.ds(x * 32 + group * tall, tall), :] for x in range(2)], axis=0
+    )
+    columns = [mine[:, layer * 8 : (layer + 1) * 8] for layer in range(8)]
+    for rank_in_group, (layer, part) in enumerate(second_order(parts)):
+        out[2 * rank_in_group : 2 * rank_in_group + 2] = columns[layer][2 * part : 2 * part + 2]
 
 
 def gram_terms(parts, scale, feats):
@@ -136,10 +159,10 @@
     examples = 2 * sources
     return pl.pallas_call(
         lambda *refs: gram_kernel(parts, deep // 2, scale, *refs),
-        out_shape=jax.ShapeDtypeStruct((8, 2 * parts, 8), F32),
+        out_shape=jax.ShapeDtypeStruct((16 * parts, 8), F32),
         in_specs=[pl.BlockSpec(memory_space=pltpu.VMEM)],
         out_specs=pl.BlockSpec(memory_space=pltpu.VMEM),
-        scratch_shapes=[pltpu.VMEM((examples, examples), F32)],
+        scratch_shapes=[pltpu.VMEM((sources * deep, lanes), F32), pltpu.VMEM((examples, examples), F32)],
         compiler_params=pltpu.CompilerParams(vmem_limit_bytes=GRAM_VMEM),
         name="gram_terms",
     )(feats.reshape(sources * deep, lanes))
@@ -152,11 +175,11 @@
     side = 2 << Z_BITS
     parts = 2 * side
     feats = features(parts, activations.reshape(count * seq, width), proj_in[0], grad_proj[0])
-    feats = lax.all_to_all(feats, "ex", 0, 0, tiled=True)
+    feats = lax.all_to_all(feats, "ex", 0, 0, axis_index_groups=[first_order()], tiled=True)
     scale = 1.0 / (seq * math.sqrt(depth * rank * rank))
     terms = gram_terms(parts, scale, feats).reshape(8 * parts, 2, 8)
     groups = [
-        [(x * 16 + z * side + w) * depth + layer for layer in range(depth) for x in range(2) for w in range(side)]
+        [(part // side * 16 + z * side + part % side) * depth + layer for layer, part in second_order(parts)]
         for z in range(16 // side)
     ]
     terms = lax.all_to_all(terms, ("ex", "layer"), 0, 0, axis_index_groups=groups, tiled=True)

time: 44.4 us -> 38 us (0.86)
  blocking collectives: 36.9 us -> 30.6 us
    all_to_all x1, blocking collectives: 17 us -> 13.1 us  [shards(): lax.all_to_all(terms, ('ex', 'layer'), 0, 0, axis_index_groups=groups, ti...]
    all_to_all x1, blocking collectives: 19.9 us -> 17.5 us  [shards(): lax.all_to_all(feats, 'ex', 0, 0, axis_index_groups=[first_order()], tile...]
where the time goes in v3:
time: 38 us; the launch traced here: 37.9 us
  blocking collectives  30.6 us (81%)
  Pallas kernels  6.6 us (17%)
  other arithmetic  0.64 us (2%)
    all_to_all x1, blocking collectives, shards(): lax.all_to_all(feats, 'ex', 0, 0, axis_index_groups=[first_order()], tile...  17.5 us
    all_to_all x1, blocking collectives, shards(): lax.all_to_all(terms, ('ex', 'layer'), 0, 0, axis_index_groups=groups, ti...  13.1 us
    pallas_call x1, Pallas kernels, features(): pl.pallas_call(lambda *refs: features_kernel(parts, *refs), out_shape=plt...  6.2 us

profile of v3, /device:TPU:1, one launch (start us, length us, event | category | flops | bytes accessed | tf_op | source)
XLA Modules:
  0.0 37.9 jit_solution(12101468895756726794)
XLA Ops:
  0.0 6.2 %features.1 = f32[32,8,128]{2,1,0:T(8,128)S(1)} custom-call(bf16[512,11008]{1,0:T(8,128)(2,1)} %bitcast.7, bf16[64,11008]{1,0:T(8,128)(2,1)} %bitcast.8, f32[2,64,256]{2,1,0:T(8,128)} %bitcast.9), custom_call_target="tpu_custom_call" | custom-call | tf_op jit(solution)/shard_map/features/pallas_call | solution.py:114
  6.2 17.5 %all_to_all.10 = f32[32,8,128]{2,1,0:T(8,128)S(1)} all-to-all(f32[32,8,128]{2,1,0:T(8,128)S(1)} %features.1), channel_id=1, replica_groups={{248,240,232,224,216,208,200,192,184,176,168,160,152,144,136,128,120,11..., dimensions={0} | all-to-all | bytes 262144 | tf_op jit(solution)/shard_map/all_to_all | solution.py:178
  23.7 0.4 %gram_terms.1 = f32[128,8]{1,0:T(8,128)S(1)} custom-call(f32[256,128]{1,0:T(8,128)S(1)} %bitcast.5), custom_call_target="tpu_custom_call" | custom-call | tf_op jit(solution)/shard_map/gram_terms/pallas_call | solution.py:160
  24.1 13.1 %all_to_all.11 = f32[64,2,8]{2,1,0:T(2,128)S(1)} all-to-all(f32[64,2,8]{2,1,0:T(2,128)S(1)} %bitcast.6), channel_id=1, replica_groups={{159,151,143,135,31,23,15,7,158,150,142,134,30,22,14,6,157,149,141,133,..., dimensions={0} | all-to-all | bytes 8192 | tf_op jit(solution)/shard_map/all_to_all | solution.py:185
  37.2 0.6 %reduce_sum.9 = f32[2,8]{1,0:T(2,128)} reduce(f32[64,2,8]{2,1,0:T(2,128)S(1)} %all_to_all.11, f32[]{:T(128)} %constant.0.clone.1), dimensions={0}, to_apply=%region_0.0 | reduce | flops 1008 | bytes 4164 | tf_op jit(solution)/shard_map/reduce_sum | solution.py:186

commit v4 on v3

--- a/solution.py
+++ b/solution.py
@@ -18,11 +18,11 @@
 
 
 def first_order():
-    return list(reversed(range(32)))
+    return [x * 16 + z * 2 + core for z in (4, 5, 6, 7, 0, 1, 2, 3) for x in (1, 0) for core in (1, 0)]
 
 
 def second_order(parts):
-    return [(layer, part) for layer in reversed(range(8)) for part in reversed(range(parts))]
+    return [(layer, part) for layer in (6, 7, 5, 4, 2, 3, 1, 0) for part in reversed(range(parts))]
 
 
 def split3(x):

time: 38 us -> 36.9 us (0.971)
  blocking collectives: 30.6 us -> 29.5 us
    all_to_all x1, blocking collectives: 17.5 us -> 16.4 us  [shards(): lax.all_to_all(feats, 'ex', 0, 0, axis_index_groups=[first_order()], tile...]
where the time goes in v4:
time: 36.9 us; the launch traced here: 36.7 us
  blocking collectives  29.5 us (80%)
  Pallas kernels  6.6 us (18%)
  other arithmetic  0.64 us (2%)
    all_to_all x1, blocking collectives, shards(): lax.all_to_all(feats, 'ex', 0, 0, axis_index_groups=[first_order()], tile...  16.4 us
    all_to_all x1, blocking collectives, shards(): lax.all_to_all(terms, ('ex', 'layer'), 0, 0, axis_index_groups=groups, ti...  13 us
    pallas_call x1, Pallas kernels, features(): pl.pallas_call(lambda *refs: features_kernel(parts, *refs), out_shape=plt...  6.2 us

profile of v4, /device:TPU:1, one launch (start us, length us, event | category | flops | bytes accessed | tf_op | source)
XLA Modules:
  0.0 36.7 jit_solution(17591393461482436485)
XLA Ops:
  0.0 6.2 %features.1 = f32[32,8,128]{2,1,0:T(8,128)S(1)} custom-call(bf16[512,11008]{1,0:T(8,128)(2,1)} %bitcast.7, bf16[64,11008]{1,0:T(8,128)(2,1)} %bitcast.8, f32[2,64,256]{2,1,0:T(8,128)} %bitcast.9), custom_call_target="tpu_custom_call" | custom-call | tf_op jit(solution)/shard_map/features/pallas_call | solution.py:114
  6.2 16.4 %all_to_all.10 = f32[32,8,128]{2,1,0:T(8,128)S(1)} all-to-all(f32[32,8,128]{2,1,0:T(8,128)S(1)} %features.1), channel_id=1, replica_groups={{200,192,72,64,216,208,88,80,232,224,104,96,248,240,120,112,136,128,8,0..., dimensions={0} | all-to-all | bytes 262144 | tf_op jit(solution)/shard_map/all_to_all | solution.py:178
  22.7 0.4 %gram_terms.1 = f32[128,8]{1,0:T(8,128)S(1)} custom-call(f32[256,128]{1,0:T(8,128)S(1)} %bitcast.5), custom_call_target="tpu_custom_call" | custom-call | tf_op jit(solution)/shard_map/gram_terms/pallas_call | solution.py:160
  23.1 13.0 %all_to_all.11 = f32[64,2,8]{2,1,0:T(2,128)S(1)} all-to-all(f32[64,2,8]{2,1,0:T(2,128)S(1)} %bitcast.6), channel_id=1, replica_groups={{158,150,142,134,30,22,14,6,159,151,143,135,31,23,15,7,157,149,141,133,..., dimensions={0} | all-to-all | bytes 8192 | tf_op jit(solution)/shard_map/all_to_all | solution.py:185
  36.1 0.6 %reduce_sum.9 = f32[2,8]{1,0:T(2,128)} reduce(f32[64,2,8]{2,1,0:T(2,128)S(1)} %all_to_all.11, f32[]{:T(128)} %constant.0.clone.1), dimensions={0}, to_apply=%region_0.0 | reduce | flops 1008 | bytes 4164 | tf_op jit(solution)/shard_map/reduce_sum | solution.py:186

commit v5 on v4

--- a/solution.py
+++ b/solution.py
@@ -132,23 +132,24 @@
     )(*(pltpu.with_memory_space_constraint(x, pltpu.HBM) for x in (acts, proj, grads)))
 
 
-def gram_kernel(parts, deep, scale, received, out, feats, gram):
-    examples = gram.shape[0]
+def gram_kernel(parts, deep, scale, received, out, feats, examples_by_share):
+    examples = examples_by_share.shape[0]
     tile = 2 * deep
     for rank_in_group, source in enumerate(first_order()):
         feats[source * tile : (source + 1) * tile] = received[rank_in_group * tile : (rank_in_group + 1) * tile]
     rows = jnp.concatenate(
         [feats[pl.ds(r, examples, stride=deep), :] for r in range(deep)], axis=1
     )
-    terms = jnp.concatenate(split3(rows), axis=0)
-    product = lax.dot_general(terms, terms, (((1,), (1,)), ((), ())), preferred_element_type=F32)
-    gram[...] = sum_blocks(product, examples, examples) * scale
+    examples_by_share[...] = rows
     side = parts // 2
     group = lax.rem(lax.axis_index("ex"), 16) // side
     tall = 2 * side
     mine = jnp.concatenate(
-        [gram[pl.ds(x * 32 + group * tall, tall), :] for x in range(2)], axis=0
+        [examples_by_share[pl.ds(x * 32 + group * tall, tall), :] for x in range(2)], axis=0
     )
+    left = jnp.concatenate(split3(mine), axis=0)
+    right = jnp.concatenate(split3(rows), axis=0)
+    mine = sum_blocks(product_of(left, right), 2 * tall, examples) * scale
     columns = [mine[:, layer * 8 : (layer + 1) * 8] for layer in range(8)]
     for rank_in_group, (layer, part) in enumerate(second_order(parts)):
         out[2 * rank_in_group : 2 * rank_in_group + 2] = columns[layer][2 * part : 2 * part + 2]
@@ -162,7 +163,7 @@
         out_shape=jax.ShapeDtypeStruct((16 * parts, 8), F32),
         in_specs=[pl.BlockSpec(memory_space=pltpu.VMEM)],
         out_specs=pl.BlockSpec(memory_space=pltpu.VMEM),
-        scratch_shapes=[pltpu.VMEM((sources * deep, lanes), F32), pltpu.VMEM((examples, examples), F32)],
+        scratch_shapes=[pltpu.VMEM((sources * deep, lanes), F32), pltpu.VMEM((examples, deep // 2 * lanes), F32)],
         compiler_params=pltpu.CompilerParams(vmem_limit_bytes=GRAM_VMEM),
         name="gram_terms",
     )(feats.reshape(sources * deep, lanes))

time: 36.9 us -> 36.8 us (level)
  no operation moved by 1% of the time
where the time goes in v5:
time: 36.8 us; the launch traced here: 36.7 us
  blocking collectives  29.5 us (80%)
  Pallas kernels  6.54 us (18%)
  other arithmetic  0.64 us (2%)
    all_to_all x1, blocking collectives, shards(): lax.all_to_all(feats, 'ex', 0, 0, axis_index_groups=[first_order()], tile...  16.4 us
    all_to_all x1, blocking collectives, shards(): lax.all_to_all(terms, ('ex', 'layer'), 0, 0, axis_index_groups=groups, ti...  13 us
    pallas_call x1, Pallas kernels, features(): pl.pallas_call(lambda *refs: features_kernel(parts, *refs), out_shape=plt...  6.2 us

profile of v5, /device:TPU:1, one launch (start us, length us, event | category | flops | bytes accessed | tf_op | source)
XLA Modules:
  0.0 36.7 jit_solution(15780717182749523159)
XLA Ops:
  0.0 6.2 %features.1 = f32[32,8,128]{2,1,0:T(8,128)S(1)} custom-call(bf16[512,11008]{1,0:T(8,128)(2,1)} %bitcast.7, bf16[64,11008]{1,0:T(8,128)(2,1)} %bitcast.8, f32[2,64,256]{2,1,0:T(8,128)} %bitcast.9), custom_call_target="tpu_custom_call" | custom-call | tf_op jit(solution)/shard_map/features/pallas_call | solution.py:114
  6.2 16.4 %all_to_all.10 = f32[32,8,128]{2,1,0:T(8,128)S(1)} all-to-all(f32[32,8,128]{2,1,0:T(8,128)S(1)} %features.1), channel_id=1, replica_groups={{200,192,72,64,216,208,88,80,232,224,104,96,248,240,120,112,136,128,8,0..., dimensions={0} | all-to-all | bytes 262144 | tf_op jit(solution)/shard_map/all_to_all | solution.py:179
  22.7 0.3 gram_terms.1
  23.0 13.0 %all_to_all.11 = f32[64,2,8]{2,1,0:T(2,128)S(1)} all-to-all(f32[64,2,8]{2,1,0:T(2,128)S(1)} %bitcast.6), channel_id=1, replica_groups={{158,150,142,134,30,22,14,6,159,151,143,135,31,23,15,7,157,149,141,133,..., dimensions={0} | all-to-all | bytes 8192 | tf_op jit(solution)/shard_map/all_to_all | solution.py:186
  36.0 0.6 %reduce_sum.9 = f32[2,8]{1,0:T(2,128)} reduce(f32[64,2,8]{2,1,0:T(2,128)S(1)} %all_to_all.11, f32[]{:T(128)} %constant.0.clone.1), dimensions={0}, to_apply=%region_0.0 | reduce | flops 1008 | bytes 4164 | tf_op jit(solution)/shard_map/reduce_sum | solution.py:187
